TPU v7x, 256 devices: a whole 4x4x8 slice. The times are simulated.
256 devices in a mesh: row: 64 (over z, x, core), col: 4 (over y).
Axes of the slice: x: 4, y: 4, z: 8, core: 2. Of those that a mesh axis runs over, the one named last changes fastest.
Arguments:
- hamiltonian: bfloat16 [18432, 128, 128], P('row'), may hold values from -0.15625 to 0.15625
- block_column: int32 [18432], P('row'), may hold values from 0 to 1535, as said below
- vectors: bfloat16 [196608, 512], P('row', 'col'), may hold values from -6 to 6
Outputs:
- filtered: bfloat16 [196608, 512], P('row', 'col')
- intersection: float32 [512, 512], P('col')
Inputs may be any that keep to these rules, and one draw needn't show every extreme that they name: Block row b's entries are block_column[b * 12 + k]. Entry k = 0 is b itself. Entries k < 10 are distinct and lie among the 24 block rows of b's own index of row (block rows i * 24 to i * 24 + 23 for i = b // 24). For k >= 10, let s = (b % 24) * 2 + k - 10 and g = s // 12; the entry lies among the block rows of index (i + o) mod 64, with o = g + 1 if g < 2, else 2 - 1 - g.
All inputs are finite; a program needn't handle non-finite values.
Results may differ from a plain program's by a relative error of at most 0.0056.
Values may be sent and summed in bfloat16 or wider, within the bound.
A program may use at most 192 MiB of HBM per device.

v0:
```python
import jax
import jax.numpy as jnp
from jax import lax
from jax.sharding import PartitionSpec as P

RPR = 2
REACH = 2
STEPS = 3
filter_center = 0.2
filter_half = 0.8


def from_behind(block, axis, distance):
    devices = range(lax.axis_size(axis))
    route = [((i - distance) % len(devices), i) for i in devices]
    return lax.ppermute(block, axis, route)


def on_device(hamiltonian, block_column, vectors):
    block_size = hamiltonian.shape[1]
    row_count = vectors.shape[0] // block_size
    width_dev = vectors.shape[1]
    per_row = hamiltonian.shape[0] // row_count
    local_count = per_row - RPR
    devices = lax.axis_size("row")
    capacity = RPR * row_count // (2 * REACH)
    offsets = [number + 1 for number in range(REACH)] + [-(number + 1) for number in range(REACH)]
    matrix_rows = hamiltonian.reshape(row_count, per_row, block_size, block_size)
    columns = block_column.reshape(row_count, per_row) % row_count
    local_index = columns[:, :local_count]
    wanted = columns[:, local_count:].reshape(2 * REACH, capacity)
    spread = jnp.arange(2 * REACH * capacity) // capacity * row_count + wanted.reshape(-1)
    remote_index = spread.reshape(row_count, RPR)

    def fetch_remote(blocks):
        stacked = jnp.concatenate(
            [from_behind(blocks, "row", -offset) for offset in offsets], axis=0
        )
        return stacked[remote_index]

    def operate(blocks):
        remote = fetch_remote(blocks)
        gathered = jnp.concatenate([blocks[local_index], remote], axis=1)
        return jnp.einsum(
            "rqij,rqjk->rik", matrix_rows, gathered, preferred_element_type=jnp.float32
        )

    previous = vectors.reshape(row_count, block_size, width_dev)
    current = (
        (operate(previous) - filter_center * previous.astype(jnp.float32)) / filter_half
    ).astype(jnp.bfloat16)
    for section in range(STEPS - 1):
        product = operate(current)
        following = (
            2.0 * (product - filter_center * current.astype(jnp.float32)) / filter_half
            - previous.astype(jnp.float32)
        ).astype(jnp.bfloat16)
        previous, current = (current, following)
    filtered = current.reshape(row_count * block_size, width_dev)
    partial_value = lax.dot_general(
        filtered,
        lax.all_gather(filtered, "col", axis=1, tiled=True),
        (((0,), (0,)), ((), ())),
        preferred_element_type=jnp.float32,
    )
    summed = lax.psum(partial_value, "row")
    return (filtered, summed / (devices * row_count * block_size))


def solution(mesh):
    return jax.shard_map(
        on_device,
        mesh=mesh,
        in_specs=(P("row", None, None), P("row"), P("row", "col")),
        out_specs=(P("row", "col"), P("col", None)),
        check_vma=False,
    )
```

profile of v0, /device:TPU:1, one launch (start us, length us, event | category | flops | bytes accessed | tf_op | source)
XLA Modules:
  0.0 386.9 jit_solution(11213303579981072683)
XLA Ops:
  11.4 4.7 %collective-permute-start.1 = (bf16[24,128,128]{2,1,0:T(8,128)(2,1)}, bf16[24,128,128]{2,1,0:T(8,128)(2,1)S(1)}, u32[]{:S(2)}, u32[]{:S(2)}) collective-permute-start(bf16[24,128,128]{2,1,0:T(8,128)(2,1)} %bitcast.35), channel_id=1, source_target_pairs={{8,0},{12,4},{16,8},{20,12},{24,16},{28,20},{32,24},{36,28},{40,32... | collective-permute-start | bytes 2359304 | tf_op jit(solution)/shard_map/ppermute | solution.py:16
  18.1 9.6 %gather_fusion = bf16[240,128,128]{2,1,0:T(8,128)(2,1)} fusion(bf16[24,128,128]{2,1,0:T(8,128)(2,1)} %bitcast.37, s32[1024]{0:T(1024)S(1)} %pad_clamp_fusion.1), kind=kCustom, calls=%fused_computation | custom fusion | bytes 15729600 | tf_op jit(solution)/shard_map/gather | solution.py:43
  27.7 5.7 %collective-permute-done.3 = bf16[24,128,128]{2,1,0:T(8,128)(2,1)S(1)} collective-permute-done((bf16[24,128,128]{2,1,0:T(8,128)(2,1)}, bf16[24,128,128]{2,1,0:T(8,128)(2,1)S(1)}, u32[]{:S(2)}, u32[]{:S(2)}) %collective-permute-start.3) | collective-permute-done | bytes 786464 | tf_op jit(solution)/shard_map/ppermute | solution.py:16
  35.4 3.9 %collective-permute-done = bf16[24,128,128]{2,1,0:T(8,128)(2,1)S(1)} collective-permute-done((bf16[24,128,128]{2,1,0:T(8,128)(2,1)}, bf16[24,128,128]{2,1,0:T(8,128)(2,1)S(1)}, u32[]{:S(2)}, u32[]{:S(2)}) %collective-permute-start) | collective-permute-done | bytes 786464 | tf_op jit(solution)/shard_map/ppermute | solution.py:16
  41.3 2.8 gather_fusion.1
  44.1 8.5 %fusion.14 = bf16[24,128,128]{2,1,0:T(8,128)(2,1)S(1)} fusion(bf16[24,128,128]{2,1,0:T(8,128)(2,1)S(1)} %bitcast.38, bf16[24,12,128,128]{3,2,1,0:T(8,128)(2,1)} %bitcast.49, bf16[24,2,128,128]{3,2,1,0:T(8,128)(2,1)S(1)} %bitcast.47, bf16[24,10,128,128]{3,2,1,0:T(8,128)(2,1)} %bitcast.41), kind=kOutput, calls=%fused_computation.27 | convolution fusion | flops 1228800000 | bytes 20447232 | tf_op jit(solution)/shard_map/rqij,rqjk->rik/dot_general | solution.py:44
  53.5 7.7 %collective-permute-start.5 = (bf16[24,128,128]{2,1,0:T(8,128)(2,1)S(1)}, bf16[24,128,128]{2,1,0:T(8,128)(2,1)}, u32[]{:S(2)}, u32[]{:S(2)}) collective-permute-start(bf16[24,128,128]{2,1,0:T(8,128)(2,1)S(1)} %fusion.14), channel_id=1, source_target_pairs={{8,0},{12,4},{16,8},{20,12},{24,16},{28,20},{32,24},{36,28},{40,32... | collective-permute-start | bytes 2359304 | tf_op jit(solution)/shard_map/ppermute | solution.py:16
  61.8 8.4 %gather_fusion.2 = bf16[240,128,128]{2,1,0:T(8,128)(2,1)} fusion(bf16[24,128,128]{2,1,0:T(8,128)(2,1)S(1)} %fusion.14, s32[1024]{0:T(1024)S(1)} %pad_clamp_fusion.1), kind=kCustom, calls=%fused_computation.2 | custom fusion | bytes 15729600 | tf_op jit(solution)/shard_map/gather | solution.py:43
  70.2 7.6 %collective-permute-done.7 = bf16[24,128,128]{2,1,0:T(8,128)(2,1)S(1)} collective-permute-done((bf16[24,128,128]{2,1,0:T(8,128)(2,1)S(1)}, bf16[24,128,128]{2,1,0:T(8,128)(2,1)S(1)}, u32[]{:S(2)}, u32[]{:S(2)}) %collective-permute-start.7) | collective-permute-done | bytes 786464 | tf_op jit(solution)/shard_map/ppermute | solution.py:16
  79.0 2.4 collective-permute-done.4
  81.4 3.0 pad_maximum_fusion.1
  84.5 3.9 gather_fusion.3
  88.4 9.0 %fusion.15 = bf16[24,128,128]{2,1,0:T(8,128)(2,1)S(1)} fusion(bf16[24,128,128]{2,1,0:T(8,128)(2,1)S(1)} %bitcast.39, bf16[24,128,128]{2,1,0:T(8,128)(2,1)S(1)} %fusion.14, bf16[24,12,128,128]{3,2,1,0:T(8,128)(2,1)} %bitcast.50, bf16[24,2,128,128]{3,2,1,0:T(8,128)(2,1)} %bitcast.48, bf16[24,10,128,128]{3,2,1,0:T(8,128)(2,1)} %bitcast.42), kind=kOutput, calls=%fused_computation.28 | convolution fusion | flops 1229586432 | bytes 21233664 | tf_op jit(solution)/shard_map/rqij,rqjk->rik/dot_general | solution.py:44
  97.4 3.0 collective-permute-start.11
  100.4 8.1 %collective-permute-start.9 = (bf16[24,128,128]{2,1,0:T(8,128)(2,1)S(1)}, bf16[24,128,128]{2,1,0:T(8,128)(2,1)}, u32[]{:S(2)}, u32[]{:S(2)}) collective-permute-start(bf16[24,128,128]{2,1,0:T(8,128)(2,1)S(1)} %fusion.15), channel_id=1, source_target_pairs={{8,0},{12,4},{16,8},{20,12},{24,16},{28,20},{32,24},{36,28},{40,32... | collective-permute-start | bytes 2359304 | tf_op jit(solution)/shard_map/ppermute | solution.py:16
  109.2 8.4 %gather_fusion.4 = bf16[240,128,128]{2,1,0:T(8,128)(2,1)} fusion(bf16[24,128,128]{2,1,0:T(8,128)(2,1)S(1)} %fusion.15, s32[1024]{0:T(1024)S(1)} %pad_clamp_fusion.1), kind=kCustom, calls=%fused_computation.4 | custom fusion | bytes 15729600 | tf_op jit(solution)/shard_map/gather | solution.py:43
  117.6 8.3 %collective-permute-done.11 = bf16[24,128,128]{2,1,0:T(8,128)(2,1)S(1)} collective-permute-done((bf16[24,128,128]{2,1,0:T(8,128)(2,1)S(1)}, bf16[24,128,128]{2,1,0:T(8,128)(2,1)S(1)}, u32[]{:S(2)}, u32[]{:S(2)}) %collective-permute-start.11) | collective-permute-done | bytes 786464 | tf_op jit(solution)/shard_map/ppermute | solution.py:16
  126.2 2.2 collective-permute-done.8
  128.4 3.0 pad_maximum_fusion.2
  131.4 3.9 gather_fusion.5
  135.3 9.9 %fusion.18 = bf16[24,128,128]{2,1,0:T(8,128)(2,1)} fusion(bf16[24,128,128]{2,1,0:T(8,128)(2,1)S(1)} %fusion.14, bf16[24,128,128]{2,1,0:T(8,128)(2,1)S(1)} %fusion.15, bf16[24,12,128,128]{3,2,1,0:T(8,128)(2,1)} %bitcast.51, bf16[24,2,128,128]{3,2,1,0:T(8,128)(2,1)} %bitcast.46, bf16[24,10,128,128]{3,2,1,0:T(8,128)(2,1)} %bitcast.40), kind=kOutput, calls=%fused_computation.31 | convolution fusion | flops 1229586432 | bytes 21233664 | tf_op jit(solution)/shard_map/rqij,rqjk->rik/dot_general | solution.py:44
  145.2 52.0 %all-gather.2.cloned.1.call-done = bf16[3072,512]{1,0:T(8,128)(2,1)} async-done(((bf16[3072,128]{1,0:T(8,128)(2,1)}), bf16[3072,512]{1,0:T(8,128)(2,1)}) %all-gather.2.cloned.1.call-update) | async-done | bytes 3145744 | tf_op jit(solution)/shard_map/all_gather | solution.py:62
  197.2 3.5 fusion.32
  200.7 177.7 %all-reduce.2.cloned.1.call-done = f32[128,512]{1,0:T(8,128)} async-done(((f32[128,512]{1,0:T(8,128)}), f32[128,512]{1,0:T(8,128)}) %all-reduce.2.cloned.1.call-update) | async-done | bytes 262160 | tf_op jit(solution)/shard_map/psum | solution.py:66
  (31 shorter events, 15.6 us)
Async XLA Ops:
  7.2 190.0 %all-gather.2.cloned.1.call-start = ((), (), s32[]{:S(2)}) async-start(), calls=%async_computation | async-start | bytes 3932160 | tf_op jit(solution)/shard_map/all_gather | solution.py:62
  7.2 26.2 %collective-permute-start.3 = (bf16[24,128,128]{2,1,0:T(8,128)(2,1)}, bf16[24,128,128]{2,1,0:T(8,128)(2,1)S(1)}, u32[]{:S(2)}, u32[]{:S(2)}) collective-permute-start(bf16[24,128,128]{2,1,0:T(8,128)(2,1)} %bitcast.33), channel_id=1, source_target_pairs={{248,0},{252,4},{0,8},{4,12},{8,16},{12,20},{16,24},{20,28},{24,32... | collective-permute-start | bytes 2359304 | tf_op jit(solution)/shard_map/ppermute | solution.py:16
  9.3 26.1 %collective-permute-start.2 = (bf16[24,128,128]{2,1,0:T(8,128)(2,1)}, bf16[24,128,128]{2,1,0:T(8,128)(2,1)S(1)}, u32[]{:S(2)}, u32[]{:S(2)}) collective-permute-start(bf16[24,128,128]{2,1,0:T(8,128)(2,1)} %bitcast.34), channel_id=1, source_target_pairs={{252,0},{0,4},{4,8},{8,12},{12,16},{16,20},{20,24},{24,28},{28,32}... | collective-permute-start | bytes 2359304 | tf_op jit(solution)/shard_map/ppermute | solution.py:16
  11.4 24.1 %collective-permute-start.1 = (bf16[24,128,128]{2,1,0:T(8,128)(2,1)}, bf16[24,128,128]{2,1,0:T(8,128)(2,1)S(1)}, u32[]{:S(2)}, u32[]{:S(2)}) collective-permute-start(bf16[24,128,128]{2,1,0:T(8,128)(2,1)} %bitcast.35), channel_id=1, source_target_pairs={{8,0},{12,4},{16,8},{20,12},{24,16},{28,20},{32,24},{36,28},{40,32... | collective-permute-start | bytes 2359304 | tf_op jit(solution)/shard_map/ppermute | solution.py:16
  16.1 23.3 %collective-permute-start = (bf16[24,128,128]{2,1,0:T(8,128)(2,1)}, bf16[24,128,128]{2,1,0:T(8,128)(2,1)S(1)}, u32[]{:S(2)}, u32[]{:S(2)}) collective-permute-start(bf16[24,128,128]{2,1,0:T(8,128)(2,1)} %bitcast.36), channel_id=1, source_target_pairs={{4,0},{8,4},{12,8},{16,12},{20,16},{24,20},{28,24},{32,28},{36,32}... | collective-permute-start | bytes 2359304 | tf_op jit(solution)/shard_map/ppermute | solution.py:16
  41.3 2.8 copy-start
  52.7 25.1 %collective-permute-start.7 = (bf16[24,128,128]{2,1,0:T(8,128)(2,1)S(1)}, bf16[24,128,128]{2,1,0:T(8,128)(2,1)S(1)}, u32[]{:S(2)}, u32[]{:S(2)}) collective-permute-start(bf16[24,128,128]{2,1,0:T(8,128)(2,1)S(1)} %fusion.14), channel_id=1, source_target_pairs={{248,0},{252,4},{0,8},{4,12},{8,16},{12,20},{16,24},{20,28},{24,32... | collective-permute-start | bytes 2359304 | tf_op jit(solution)/shard_map/ppermute | solution.py:16
  53.2 25.8 %collective-permute-start.6 = (bf16[24,128,128]{2,1,0:T(8,128)(2,1)S(1)}, bf16[24,128,128]{2,1,0:T(8,128)(2,1)S(1)}, u32[]{:S(2)}, u32[]{:S(2)}) collective-permute-start(bf16[24,128,128]{2,1,0:T(8,128)(2,1)S(1)} %fusion.14), channel_id=1, source_target_pairs={{252,0},{0,4},{4,8},{8,12},{12,16},{16,20},{20,24},{24,28},{28,32}... | collective-permute-start | bytes 2359304 | tf_op jit(solution)/shard_map/ppermute | solution.py:16
  53.5 25.6 %collective-permute-start.5 = (bf16[24,128,128]{2,1,0:T(8,128)(2,1)S(1)}, bf16[24,128,128]{2,1,0:T(8,128)(2,1)}, u32[]{:S(2)}, u32[]{:S(2)}) collective-permute-start(bf16[24,128,128]{2,1,0:T(8,128)(2,1)S(1)} %fusion.14), channel_id=1, source_target_pairs={{8,0},{12,4},{16,8},{20,12},{24,16},{28,20},{32,24},{36,28},{40,32... | collective-permute-start | bytes 2359304 | tf_op jit(solution)/shard_map/ppermute | solution.py:16
  61.2 20.3 %collective-permute-start.4 = (bf16[24,128,128]{2,1,0:T(8,128)(2,1)S(1)}, bf16[24,128,128]{2,1,0:T(8,128)(2,1)}, u32[]{:S(2)}, u32[]{:S(2)}) collective-permute-start(bf16[24,128,128]{2,1,0:T(8,128)(2,1)S(1)} %fusion.14), channel_id=1, source_target_pairs={{4,0},{8,4},{12,8},{16,12},{20,16},{24,20},{28,24},{32,28},{36,32}... | collective-permute-start | bytes 2359304 | tf_op jit(solution)/shard_map/ppermute | solution.py:16
  97.4 28.5 %collective-permute-start.11 = (bf16[24,128,128]{2,1,0:T(8,128)(2,1)S(1)}, bf16[24,128,128]{2,1,0:T(8,128)(2,1)S(1)}, u32[]{:S(2)}, u32[]{:S(2)}) collective-permute-start(bf16[24,128,128]{2,1,0:T(8,128)(2,1)S(1)} %fusion.15), channel_id=1, source_target_pairs={{248,0},{252,4},{0,8},{4,12},{8,16},{12,20},{16,24},{20,28},{24,32... | collective-permute-start | bytes 2359304 | tf_op jit(solution)/shard_map/ppermute | solution.py:16
  100.4 25.8 %collective-permute-start.10 = (bf16[24,128,128]{2,1,0:T(8,128)(2,1)S(1)}, bf16[24,128,128]{2,1,0:T(8,128)(2,1)S(1)}, u32[]{:S(2)}, u32[]{:S(2)}) collective-permute-start(bf16[24,128,128]{2,1,0:T(8,128)(2,1)S(1)} %fusion.15), channel_id=1, source_target_pairs={{252,0},{0,4},{4,8},{8,12},{12,16},{16,20},{20,24},{24,28},{28,32}... | collective-permute-start | bytes 2359304 | tf_op jit(solution)/shard_map/ppermute | solution.py:16
  100.4 25.8 %collective-permute-start.9 = (bf16[24,128,128]{2,1,0:T(8,128)(2,1)S(1)}, bf16[24,128,128]{2,1,0:T(8,128)(2,1)}, u32[]{:S(2)}, u32[]{:S(2)}) collective-permute-start(bf16[24,128,128]{2,1,0:T(8,128)(2,1)S(1)} %fusion.15), channel_id=1, source_target_pairs={{8,0},{12,4},{16,8},{20,12},{24,16},{28,20},{32,24},{36,28},{40,32... | collective-permute-start | bytes 2359304 | tf_op jit(solution)/shard_map/ppermute | solution.py:16
  108.5 19.9 %collective-permute-start.8 = (bf16[24,128,128]{2,1,0:T(8,128)(2,1)S(1)}, bf16[24,128,128]{2,1,0:T(8,128)(2,1)}, u32[]{:S(2)}, u32[]{:S(2)}) collective-permute-start(bf16[24,128,128]{2,1,0:T(8,128)(2,1)S(1)} %fusion.15), channel_id=1, source_target_pairs={{4,0},{8,4},{12,8},{16,12},{20,16},{24,20},{28,24},{32,28},{36,32}... | collective-permute-start | bytes 2359304 | tf_op jit(solution)/shard_map/ppermute | solution.py:16
  145.2 233.2 %all-reduce.2.cloned.1.call-start = ((), (), s32[]{:S(2)}) async-start(), calls=%async_computation.1 | async-start | bytes 524288 | tf_op jit(solution)/shard_map/psum | solution.py:66
Sparse Core Ops, SparseCore 0:
  145.3 51.8 all-gather.1
  201.3 177.0 all-reduce.1
where the time goes:
time: 387 us
  waiting for transfers between devices  263 us (68%)
  local copies, waits for them, and re-layouts  37.2 us (10%)
  matrix products  30.9 us (8%)
  starting transfers between devices  30.8 us (8%)
  between operations  14.1 us (4%)
  other arithmetic  10.5 us (3%)
    psum x1, waiting for transfers between devices, on_device(): summed = lax.psum(partial_value, 'row')  178 us
    all_gather x1, waiting for transfers between devices, on_device(): lax.all_gather(filtered, 'col', axis=1, tiled=True)  52 us
    ppermute x12, waiting for transfers between devices, from_behind(): return lax.ppermute(block, axis, route)  33.7 us
    ppermute x12, starting transfers between devices, from_behind(): return lax.ppermute(block, axis, route)  30.7 us
    dot_general x3, matrix products, operate(): jnp.einsum('rqij,rqjk->rik', matrix_rows, gathered, preferred_element_typ...  27.4 us
    gather x3, local copies, waits for them, and re-layouts, operate(): gathered = jnp.concatenate([blocks[local_index], remote], axis=1)  26.4 us
    gather x3, local copies, waits for them, and re-layouts, fetch_remote(): return stacked[remote_index]  10.5 us
    concatenate x3, other arithmetic, fetch_remote(): jnp.concatenate([from_behind(blocks, 'row', -offset) for offset in offset...  8.01 us
  transfers between devices with their start and end apart: 14, of which 11 were waited for; matrix products, arithmetic and copies ran while one was open for 7% of the time, Pallas kernels for 0%

commit v1 on v0

--- a/solution.py
+++ b/solution.py
@@ -8,6 +8,17 @@
 STEPS = 3
 filter_center = 0.2
 filter_half = 0.8
+
+
+def gather_around(x, axis, dim):
+    ways = lax.axis_size(axis)
+    pieces = [x]
+    for far in range(1, ways):
+        pieces.append(
+            lax.ppermute(pieces[far - 1], axis, [(d, (d - 1) % ways) for d in range(ways)])
+        )
+    line = jnp.concatenate(pieces, axis=dim)
+    return jnp.roll(line, lax.axis_index(axis) * x.shape[dim], axis=dim)
 
 
 def from_behind(block, axis, distance):
@@ -59,7 +70,7 @@
     filtered = current.reshape(row_count * block_size, width_dev)
     partial_value = lax.dot_general(
         filtered,
-        lax.all_gather(filtered, "col", axis=1, tiled=True),
+        gather_around(filtered, "col", 1),
         (((0,), (0,)), ((), ())),
         preferred_element_type=jnp.float32,
     )

time: 387 us -> 399 us (1.031)
  starting transfers between devices: 30.8 us -> 40.4 us
    all_gather x1 -> x0, waiting for transfers between devices: 52 us -> none  [on_device(): lax.all_gather(filtered, 'col', axis=1, tiled=True)]
    ppermute x0 -> x3, waiting for transfers between devices: none -> 35 us  [gather_around(): lax.ppermute(pieces[far - 1], axis, [(d, (d - 1) % ways) for d in range(w...]
    psum x1, waiting for transfers between devices: 178 us -> 196 us  [on_device(): summed = lax.psum(partial_value, 'row')]
    ppermute x0 -> x3, starting transfers between devices: none -> 9.63 us  [gather_around(): lax.ppermute(pieces[far - 1], axis, [(d, (d - 1) % ways) for d in range(w...]
  transfers between devices with their start and end apart: 14 -> 16, of which waited for: 11 -> 13; matrix products, arithmetic and copies ran while one was open for 7% -> 7% of each run, Pallas kernels for 0% -> 0%
where the time goes in v1:
time: 399 us; the launch traced here: 398 us
  waiting for transfers between devices  265 us (66%)
  starting transfers between devices  40.4 us (10%)
  local copies, waits for them, and re-layouts  39.2 us (10%)
  matrix products  27.9 us (7%)
  between operations  14.2 us (4%)
  other arithmetic  11.5 us (3%)
    psum x1, waiting for transfers between devices, on_device(): summed = lax.psum(partial_value, 'row')  196 us
    ppermute x3, waiting for transfers between devices, gather_around(): lax.ppermute(pieces[far - 1], axis, [(d, (d - 1) % ways) for d in range(w...  35 us
    ppermute x12, waiting for transfers between devices, from_behind(): return lax.ppermute(block, axis, route)  33.8 us
    ppermute x12, starting transfers between devices, from_behind(): return lax.ppermute(block, axis, route)  30.7 us
    dot_general x3, matrix products, operate(): jnp.einsum('rqij,rqjk->rik', matrix_rows, gathered, preferred_element_typ...  26.5 us
    gather x3, local copies, waits for them, and re-layouts, operate(): gathered = jnp.concatenate([blocks[local_index], remote], axis=1)  26.4 us
    gather x3, local copies, waits for them, and re-layouts, fetch_remote(): return stacked[remote_index]  10.5 us
    ppermute x3, starting transfers between devices, gather_around(): lax.ppermute(pieces[far - 1], axis, [(d, (d - 1) % ways) for d in range(w...  9.63 us
  transfers between devices with their start and end apart: 16, of which 13 were waited for; matrix products, arithmetic and copies ran while one was open for 7% of the time, Pallas kernels for 0%

profile of v1, /device:TPU:1, one launch (start us, length us, event | category | flops | bytes accessed | tf_op | source)
XLA Modules:
  0.0 398.2 jit_solution(15696263950553481475)
XLA Ops:
  11.4 4.7 %collective-permute-start.1 = (bf16[24,128,128]{2,1,0:T(8,128)(2,1)}, bf16[24,128,128]{2,1,0:T(8,128)(2,1)S(1)}, u32[]{:S(2)}, u32[]{:S(2)}) collective-permute-start(bf16[24,128,128]{2,1,0:T(8,128)(2,1)} %bitcast.34), channel_id=1, source_target_pairs={{8,0},{12,4},{16,8},{20,12},{24,16},{28,20},{32,24},{36,28},{40,32... | collective-permute-start | bytes 2359304 | tf_op jit(solution)/shard_map/ppermute | solution.py:27
  18.1 9.5 %gather_fusion = bf16[240,128,128]{2,1,0:T(8,128)(2,1)} fusion(bf16[24,128,128]{2,1,0:T(8,128)(2,1)} %bitcast.36, s32[1024]{0:T(1024)S(1)} %pad_clamp_fusion.1), kind=kCustom, calls=%fused_computation | custom fusion | bytes 15729600 | tf_op jit(solution)/shard_map/gather | solution.py:54
  27.7 5.7 %collective-permute-done.3 = bf16[24,128,128]{2,1,0:T(8,128)(2,1)S(1)} collective-permute-done((bf16[24,128,128]{2,1,0:T(8,128)(2,1)}, bf16[24,128,128]{2,1,0:T(8,128)(2,1)S(1)}, u32[]{:S(2)}, u32[]{:S(2)}) %collective-permute-start.3) | collective-permute-done | bytes 786464 | tf_op jit(solution)/shard_map/ppermute | solution.py:27
  35.4 3.9 collective-permute-done
  45.1 8.5 %fusion.16 = bf16[24,128,128]{2,1,0:T(8,128)(2,1)S(1)} fusion(bf16[24,128,128]{2,1,0:T(8,128)(2,1)S(1)} %bitcast.37, bf16[24,12,128,128]{3,2,1,0:T(8,128)(2,1)} %bitcast.50, bf16[24,2,128,128]{3,2,1,0:T(8,128)(2,1)S(1)} %bitcast.48, bf16[24,10,128,128]{3,2,1,0:T(8,128)(2,1)} %bitcast.40), kind=kOutput, calls=%fused_computation.29 | convolution fusion | flops 1228800000 | bytes 20447232 | tf_op jit(solution)/shard_map/rqij,rqjk->rik/dot_general | solution.py:55
  54.4 7.7 %collective-permute-start.5 = (bf16[24,128,128]{2,1,0:T(8,128)(2,1)S(1)}, bf16[24,128,128]{2,1,0:T(8,128)(2,1)}, u32[]{:S(2)}, u32[]{:S(2)}) collective-permute-start(bf16[24,128,128]{2,1,0:T(8,128)(2,1)S(1)} %fusion.16), channel_id=1, source_target_pairs={{8,0},{12,4},{16,8},{20,12},{24,16},{28,20},{32,24},{36,28},{40,32... | collective-permute-start | bytes 2359304 | tf_op jit(solution)/shard_map/ppermute | solution.py:27
  62.7 8.4 %gather_fusion.2 = bf16[240,128,128]{2,1,0:T(8,128)(2,1)} fusion(bf16[24,128,128]{2,1,0:T(8,128)(2,1)S(1)} %fusion.16, s32[1024]{0:T(1024)S(1)} %pad_clamp_fusion.1), kind=kCustom, calls=%fused_computation.2 | custom fusion | bytes 15729600 | tf_op jit(solution)/shard_map/gather | solution.py:54
  71.1 7.8 %collective-permute-done.7 = bf16[24,128,128]{2,1,0:T(8,128)(2,1)S(1)} collective-permute-done((bf16[24,128,128]{2,1,0:T(8,128)(2,1)S(1)}, bf16[24,128,128]{2,1,0:T(8,128)(2,1)S(1)}, u32[]{:S(2)}, u32[]{:S(2)}) %collective-permute-start.7) | collective-permute-done | bytes 786464 | tf_op jit(solution)/shard_map/ppermute | solution.py:27
  82.4 3.1 pad_maximum_fusion.1
  85.5 3.9 gather_fusion.3
  89.3 9.0 %fusion.17 = bf16[24,128,128]{2,1,0:T(8,128)(2,1)S(1)} fusion(bf16[24,128,128]{2,1,0:T(8,128)(2,1)S(1)} %bitcast.38, bf16[24,128,128]{2,1,0:T(8,128)(2,1)S(1)} %fusion.16, bf16[24,12,128,128]{3,2,1,0:T(8,128)(2,1)} %bitcast.51, bf16[24,2,128,128]{3,2,1,0:T(8,128)(2,1)} %bitcast.49, bf16[24,10,128,128]{3,2,1,0:T(8,128)(2,1)} %bitcast.41), kind=kOutput, calls=%fused_computation.30 | convolution fusion | flops 1229586432 | bytes 21233664 | tf_op jit(solution)/shard_map/rqij,rqjk->rik/dot_general | solution.py:55
  98.3 3.0 collective-permute-start.11
  101.4 8.1 %collective-permute-start.9 = (bf16[24,128,128]{2,1,0:T(8,128)(2,1)S(1)}, bf16[24,128,128]{2,1,0:T(8,128)(2,1)}, u32[]{:S(2)}, u32[]{:S(2)}) collective-permute-start(bf16[24,128,128]{2,1,0:T(8,128)(2,1)S(1)} %fusion.17), channel_id=1, source_target_pairs={{8,0},{12,4},{16,8},{20,12},{24,16},{28,20},{32,24},{36,28},{40,32... | collective-permute-start | bytes 2359304 | tf_op jit(solution)/shard_map/ppermute | solution.py:27
  110.1 8.4 %gather_fusion.4 = bf16[240,128,128]{2,1,0:T(8,128)(2,1)} fusion(bf16[24,128,128]{2,1,0:T(8,128)(2,1)S(1)} %fusion.17, s32[1024]{0:T(1024)S(1)} %pad_clamp_fusion.1), kind=kCustom, calls=%fused_computation.4 | custom fusion | bytes 15729600 | tf_op jit(solution)/shard_map/gather | solution.py:54
  118.5 8.2 %collective-permute-done.11 = bf16[24,128,128]{2,1,0:T(8,128)(2,1)S(1)} collective-permute-done((bf16[24,128,128]{2,1,0:T(8,128)(2,1)S(1)}, bf16[24,128,128]{2,1,0:T(8,128)(2,1)S(1)}, u32[]{:S(2)}, u32[]{:S(2)}) %collective-permute-start.11) | collective-permute-done | bytes 786464 | tf_op jit(solution)/shard_map/ppermute | solution.py:27
  129.3 3.1 pad_maximum_fusion.2
  132.4 3.9 gather_fusion.5
  136.3 9.0 %fusion.20 = bf16[24,128,128]{2,1,0:T(8,128)(2,1)S(1)} fusion(bf16[24,128,128]{2,1,0:T(8,128)(2,1)S(1)} %fusion.16, bf16[24,128,128]{2,1,0:T(8,128)(2,1)S(1)} %fusion.17, bf16[24,12,128,128]{3,2,1,0:T(8,128)(2,1)} %bitcast.52, bf16[24,2,128,128]{3,2,1,0:T(8,128)(2,1)} %bitcast.47, bf16[24,10,128,128]{3,2,1,0:T(8,128)(2,1)} %bitcast.39), kind=kOutput, calls=%fused_computation.33 | convolution fusion | flops 1229586432 | bytes 21233664 | tf_op jit(solution)/shard_map/rqij,rqjk->rik/dot_general | solution.py:55
  148.1 10.0 %collective-permute-done.12 = bf16[3072,128]{1,0:T(8,128)(2,1)S(1)} collective-permute-done((bf16[3072,128]{1,0:T(8,128)(2,1)S(1)}, bf16[3072,128]{1,0:T(8,128)(2,1)S(1)}, u32[]{:S(2)}, u32[]{:S(2)}) %collective-permute-start.12) | collective-permute-done | bytes 786464 | tf_op jit(solution)/shard_map/ppermute | solution.py:18
  158.1 3.4 collective-permute-start.13
  161.5 12.6 %collective-permute-done.13 = bf16[3072,128]{1,0:T(8,128)(2,1)S(1)} collective-permute-done((bf16[3072,128]{1,0:T(8,128)(2,1)S(1)}, bf16[3072,128]{1,0:T(8,128)(2,1)S(1)}, u32[]{:S(2)}, u32[]{:S(2)}) %collective-permute-start.13) | collective-permute-done | bytes 786464 | tf_op jit(solution)/shard_map/ppermute | solution.py:18
  174.1 3.4 collective-permute-start.14
  178.3 12.4 %collective-permute-done.14 = bf16[3072,128]{1,0:T(8,128)(2,1)S(1)} collective-permute-done((bf16[3072,128]{1,0:T(8,128)(2,1)S(1)}, bf16[3072,128]{1,0:T(8,128)(2,1)S(1)}, u32[]{:S(2)}, u32[]{:S(2)}) %collective-permute-start.14) | collective-permute-done | bytes 786464 | tf_op jit(solution)/shard_map/ppermute | solution.py:18
  193.5 196.2 %all-reduce.2.cloned.1.call-done = f32[128,512]{1,0:T(8,128)} async-done(((f32[128,512]{1,0:T(8,128)}), f32[128,512]{1,0:T(8,128)}) %all-reduce.2.cloned.1.call-update) | async-done | bytes 262160 | tf_op jit(solution)/shard_map/psum | solution.py:77
  (44 shorter events, 30.1 us)
Async XLA Ops:
  7.2 382.5 %all-reduce.2.cloned.1.call-start = ((), (), s32[]{:S(2)}) async-start(), calls=%async_computation | async-start | bytes 524288 | tf_op jit(solution)/shard_map/psum | solution.py:77
  7.2 26.2 %collective-permute-start.3 = (bf16[24,128,128]{2,1,0:T(8,128)(2,1)}, bf16[24,128,128]{2,1,0:T(8,128)(2,1)S(1)}, u32[]{:S(2)}, u32[]{:S(2)}) collective-permute-start(bf16[24,128,128]{2,1,0:T(8,128)(2,1)} %bitcast.32), channel_id=1, source_target_pairs={{248,0},{252,4},{0,8},{4,12},{8,16},{12,20},{16,24},{20,28},{24,32... | collective-permute-start | bytes 2359304 | tf_op jit(solution)/shard_map/ppermute | solution.py:27
  9.3 26.1 %collective-permute-start.2 = (bf16[24,128,128]{2,1,0:T(8,128)(2,1)}, bf16[24,128,128]{2,1,0:T(8,128)(2,1)S(1)}, u32[]{:S(2)}, u32[]{:S(2)}) collective-permute-start(bf16[24,128,128]{2,1,0:T(8,128)(2,1)} %bitcast.33), channel_id=1, source_target_pairs={{252,0},{0,4},{4,8},{8,12},{12,16},{16,20},{20,24},{24,28},{28,32}... | collective-permute-start | bytes 2359304 | tf_op jit(solution)/shard_map/ppermute | solution.py:27
  11.4 24.1 %collective-permute-start.1 = (bf16[24,128,128]{2,1,0:T(8,128)(2,1)}, bf16[24,128,128]{2,1,0:T(8,128)(2,1)S(1)}, u32[]{:S(2)}, u32[]{:S(2)}) collective-permute-start(bf16[24,128,128]{2,1,0:T(8,128)(2,1)} %bitcast.34), channel_id=1, source_target_pairs={{8,0},{12,4},{16,8},{20,12},{24,16},{28,20},{32,24},{36,28},{40,32... | collective-permute-start | bytes 2359304 | tf_op jit(solution)/shard_map/ppermute | solution.py:27
  16.1 23.3 %collective-permute-start = (bf16[24,128,128]{2,1,0:T(8,128)(2,1)}, bf16[24,128,128]{2,1,0:T(8,128)(2,1)}, u32[]{:S(2)}, u32[]{:S(2)}) collective-permute-start(bf16[24,128,128]{2,1,0:T(8,128)(2,1)} %bitcast.35), channel_id=1, source_target_pairs={{4,0},{8,4},{12,8},{16,12},{20,16},{24,20},{28,24},{32,28},{36,32}... | collective-permute-start | bytes 2359304 | tf_op jit(solution)/shard_map/ppermute | solution.py:27
  27.7 17.4 %copy-start = (bf16[3072,128]{1,0:T(8,128)(2,1)S(1)}, bf16[3072,128]{1,0:T(8,128)(2,1)}, u32[]{:S(2)}) copy-start(bf16[3072,128]{1,0:T(8,128)(2,1)} %param.5) | copy-start | bytes 2359300
  53.6 25.3 %collective-permute-start.7 = (bf16[24,128,128]{2,1,0:T(8,128)(2,1)S(1)}, bf16[24,128,128]{2,1,0:T(8,128)(2,1)S(1)}, u32[]{:S(2)}, u32[]{:S(2)}) collective-permute-start(bf16[24,128,128]{2,1,0:T(8,128)(2,1)S(1)} %fusion.16), channel_id=1, source_target_pairs={{248,0},{252,4},{0,8},{4,12},{8,16},{12,20},{16,24},{20,28},{24,32... | collective-permute-start | bytes 2359304 | tf_op jit(solution)/shard_map/ppermute | solution.py:27
  54.3 25.8 %collective-permute-start.6 = (bf16[24,128,128]{2,1,0:T(8,128)(2,1)S(1)}, bf16[24,128,128]{2,1,0:T(8,128)(2,1)S(1)}, u32[]{:S(2)}, u32[]{:S(2)}) collective-permute-start(bf16[24,128,128]{2,1,0:T(8,128)(2,1)S(1)} %fusion.16), channel_id=1, source_target_pairs={{252,0},{0,4},{4,8},{8,12},{12,16},{16,20},{20,24},{24,28},{28,32}... | collective-permute-start | bytes 2359304 | tf_op jit(solution)/shard_map/ppermute | solution.py:27
  54.4 25.7 %collective-permute-start.5 = (bf16[24,128,128]{2,1,0:T(8,128)(2,1)S(1)}, bf16[24,128,128]{2,1,0:T(8,128)(2,1)}, u32[]{:S(2)}, u32[]{:S(2)}) collective-permute-start(bf16[24,128,128]{2,1,0:T(8,128)(2,1)S(1)} %fusion.16), channel_id=1, source_target_pairs={{8,0},{12,4},{16,8},{20,12},{24,16},{28,20},{32,24},{36,28},{40,32... | collective-permute-start | bytes 2359304 | tf_op jit(solution)/shard_map/ppermute | solution.py:27
  62.1 20.3 %collective-permute-start.4 = (bf16[24,128,128]{2,1,0:T(8,128)(2,1)S(1)}, bf16[24,128,128]{2,1,0:T(8,128)(2,1)}, u32[]{:S(2)}, u32[]{:S(2)}) collective-permute-start(bf16[24,128,128]{2,1,0:T(8,128)(2,1)S(1)} %fusion.16), channel_id=1, source_target_pairs={{4,0},{8,4},{12,8},{16,12},{20,16},{24,20},{28,24},{32,28},{36,32}... | collective-permute-start | bytes 2359304 | tf_op jit(solution)/shard_map/ppermute | solution.py:27
  98.3 28.4 %collective-permute-start.11 = (bf16[24,128,128]{2,1,0:T(8,128)(2,1)S(1)}, bf16[24,128,128]{2,1,0:T(8,128)(2,1)S(1)}, u32[]{:S(2)}, u32[]{:S(2)}) collective-permute-start(bf16[24,128,128]{2,1,0:T(8,128)(2,1)S(1)} %fusion.17), channel_id=1, source_target_pairs={{248,0},{252,4},{0,8},{4,12},{8,16},{12,20},{16,24},{20,28},{24,32... | collective-permute-start | bytes 2359304 | tf_op jit(solution)/shard_map/ppermute | solution.py:27
  101.3 25.8 %collective-permute-start.10 = (bf16[24,128,128]{2,1,0:T(8,128)(2,1)S(1)}, bf16[24,128,128]{2,1,0:T(8,128)(2,1)S(1)}, u32[]{:S(2)}, u32[]{:S(2)}) collective-permute-start(bf16[24,128,128]{2,1,0:T(8,128)(2,1)S(1)} %fusion.17), channel_id=1, source_target_pairs={{252,0},{0,4},{4,8},{8,12},{12,16},{16,20},{20,24},{24,28},{28,32}... | collective-permute-start | bytes 2359304 | tf_op jit(solution)/shard_map/ppermute | solution.py:27
  101.4 25.8 %collective-permute-start.9 = (bf16[24,128,128]{2,1,0:T(8,128)(2,1)S(1)}, bf16[24,128,128]{2,1,0:T(8,128)(2,1)}, u32[]{:S(2)}, u32[]{:S(2)}) collective-permute-start(bf16[24,128,128]{2,1,0:T(8,128)(2,1)S(1)} %fusion.17), channel_id=1, source_target_pairs={{8,0},{12,4},{16,8},{20,12},{24,16},{28,20},{32,24},{36,28},{40,32... | collective-permute-start | bytes 2359304 | tf_op jit(solution)/shard_map/ppermute | solution.py:27
  109.4 19.9 %collective-permute-start.8 = (bf16[24,128,128]{2,1,0:T(8,128)(2,1)S(1)}, bf16[24,128,128]{2,1,0:T(8,128)(2,1)}, u32[]{:S(2)}, u32[]{:S(2)}) collective-permute-start(bf16[24,128,128]{2,1,0:T(8,128)(2,1)S(1)} %fusion.17), channel_id=1, source_target_pairs={{4,0},{8,4},{12,8},{16,12},{20,16},{24,20},{28,24},{32,28},{36,32}... | collective-permute-start | bytes 2359304 | tf_op jit(solution)/shard_map/ppermute | solution.py:27
  145.3 46.9 %copy-start.1 = (bf16[24,128,128]{2,1,0:T(8,128)(2,1)}, bf16[24,128,128]{2,1,0:T(8,128)(2,1)S(1)}, u32[]{:S(2)}) copy-start(bf16[24,128,128]{2,1,0:T(8,128)(2,1)S(1)} %fusion.20) | copy-start | bytes 2359300
  145.3 12.8 %collective-permute-start.12 = (bf16[3072,128]{1,0:T(8,128)(2,1)S(1)}, bf16[3072,128]{1,0:T(8,128)(2,1)S(1)}, u32[]{:S(2)}, u32[]{:S(2)}) collective-permute-start(bf16[3072,128]{1,0:T(8,128)(2,1)S(1)} %bitcast.42), channel_id=1, source_target_pairs={{0,3},{1,0},{2,1},{3,2},{4,7},{5,4},{6,5},{7,6},{8,11},{9,8},{10,9... | collective-permute-start | bytes 2359304 | tf_op jit(solution)/shard_map/ppermute | solution.py:18
  158.1 16.0 %collective-permute-start.13 = (bf16[3072,128]{1,0:T(8,128)(2,1)S(1)}, bf16[3072,128]{1,0:T(8,128)(2,1)S(1)}, u32[]{:S(2)}, u32[]{:S(2)}) collective-permute-start(bf16[3072,128]{1,0:T(8,128)(2,1)S(1)} %collective-permute-done.12), channel_id=1, source_target_pairs={{0,3},{1,0},{2,1},{3,2},{4,7},{5,4},{6,5},{7,6},{8,11},{9,8},{10,9... | collective-permute-start | bytes 2359304 | tf_op jit(solution)/shard_map/ppermute | solution.py:18
  174.1 16.6 %collective-permute-start.14 = (bf16[3072,128]{1,0:T(8,128)(2,1)S(1)}, bf16[3072,128]{1,0:T(8,128)(2,1)S(1)}, u32[]{:S(2)}, u32[]{:S(2)}) collective-permute-start(bf16[3072,128]{1,0:T(8,128)(2,1)S(1)} %collective-permute-done.13), channel_id=1, source_target_pairs={{0,3},{1,0},{2,1},{3,2},{4,7},{5,4},{6,5},{7,6},{8,11},{9,8},{10,9... | collective-permute-start | bytes 2359304 | tf_op jit(solution)/shard_map/ppermute | solution.py:18
Sparse Core Ops, SparseCore 0:
  193.6 196.0 all-reduce.1
